TPU v7x, 256 devices: a whole 4x4x8 slice. The times are simulated.
256 devices in a mesh: gx: 8 (over z_hi, core), gy: 4 (over x), gz: 8 (over z_lo, y).
Axes of the slice: x: 4, y: 4, z: 8 (z_hi: 4, z_lo: 2; z = z_hi * 2 + z_lo), core: 2. Of those that a mesh axis runs over, the one named last changes fastest.
Arguments:
- tokens: bfloat16 [1024, 8192], P('gy', ('gz', 'gx')), may hold values from -6 to 6
- gate_weight: bfloat16 [8192, 14336], P('gz', ('gx', 'gy')), may hold values from -0.0625 to 0.0625
- up_weight: bfloat16 [8192, 14336], P('gz', ('gx', 'gy')), may hold values from -0.0625 to 0.0625
- down_weight: bfloat16 [14336, 8192], P('gx', ('gz', 'gy')), may hold values from -0.046875 to 0.046875
- out_grad: bfloat16 [1024, 8192], P('gy', ('gz', 'gx')), may hold values from -6 to 6
Outputs:
- mixed: bfloat16 [1024, 8192], P('gy', ('gz', 'gx'))
- tokens_grad: bfloat16 [1024, 8192], P('gy', ('gz', 'gx'))
- gate_grad: bfloat16 [8192, 14336], P('gz', ('gx', 'gy'))
- up_grad: bfloat16 [8192, 14336], P('gz', ('gx', 'gy'))
- down_grad: bfloat16 [14336, 8192], P('gx', ('gz', 'gy'))
All inputs are finite; a program needn't handle non-finite values.
Results may differ from a plain program's by a relative error of at most 0.0049.
Values may be sent and summed in bfloat16 or wider, within the bound.
No kernel may reach another device: no remote copies, remote signals or barrier semaphores. Data moves between devices by JAX's collectives and lax.ppermute only.
A program may use at most 128 MiB of HBM per device.

v0:
```python
import jax
import jax.numpy as jnp
from jax import lax
from jax.sharding import PartitionSpec as P


def matmul(left, right):
    return jnp.dot(left, right, preferred_element_type=jnp.float32)


def matmul_right_t(left, right):
    return lax.dot_general(
        left, right, (((1,), (1,)), ((), ())), preferred_element_type=jnp.float32
    )


def matmul_left_t(left, right):
    return lax.dot_general(
        left, right, (((0,), (0,)), ((), ())), preferred_element_type=jnp.float32
    )


def local(tokens, gate_weight, up_weight, down_weight, out_grad):
    tok_cols, grad_cols = (
        lax.all_gather(tokens, "gx", axis=1, tiled=True),
        lax.all_gather(out_grad, "gx", axis=1, tiled=True),
    )
    gate_full, up_full, down_full = (
        lax.all_gather(gate_weight, "gy", axis=1, tiled=True),
        lax.all_gather(up_weight, "gy", axis=1, tiled=True),
        lax.all_gather(down_weight, "gy", axis=1, tiled=True),
    )
    gate_part = matmul(tok_cols, gate_full)
    up_part = matmul(tok_cols, up_full)
    gate_rows, up_rows = (
        lax.psum_scatter(gate_part, "gz", scatter_dimension=0, tiled=True),
        lax.psum_scatter(up_part, "gz", scatter_dimension=0, tiled=True),
    )
    sig = jax.nn.sigmoid(gate_rows)
    act = gate_rows * sig
    hidden = (act * up_rows).astype(jnp.bfloat16)
    hidden_all = lax.all_gather(hidden, "gz", axis=0, tiled=True)
    out_part = matmul(hidden_all, down_full)
    mixed = lax.psum_scatter(out_part, "gx", scatter_dimension=1, tiled=True).astype(jnp.bfloat16)
    dh_part = matmul_right_t(grad_cols, down_full)
    dh_rows = lax.psum_scatter(dh_part, "gz", scatter_dimension=0, tiled=True)
    gate_delta = (dh_rows * up_rows * sig * (1.0 + gate_rows * (1.0 - sig))).astype(jnp.bfloat16)
    up_delta = (dh_rows * act).astype(jnp.bfloat16)
    gate_all, up_all = (
        lax.all_gather(gate_delta, "gz", axis=0, tiled=True),
        lax.all_gather(up_delta, "gz", axis=0, tiled=True),
    )
    dx_part = matmul_right_t(gate_all, gate_full) + matmul_right_t(up_all, up_full)
    tokens_grad = lax.psum_scatter(dx_part, "gx", scatter_dimension=1, tiled=True).astype(
        jnp.bfloat16
    )
    delta_gate, delta_up, grad_slice = (
        lax.all_to_all(gate_all, "gy", split_axis=1, concat_axis=0, tiled=True),
        lax.all_to_all(up_all, "gy", split_axis=1, concat_axis=0, tiled=True),
        lax.all_to_all(grad_cols, "gy", split_axis=1, concat_axis=0, tiled=True),
    )
    pieces = (
        lax.all_gather(tok_cols, "gy", axis=0, tiled=True),
        lax.all_gather(hidden_all, "gy", axis=0, tiled=True),
    )
    gate_grad = matmul_left_t(pieces[0], delta_gate)
    up_grad = matmul_left_t(pieces[0], delta_up)
    down_grad = matmul_left_t(pieces[1], grad_slice)
    return (
        mixed,
        tokens_grad,
        gate_grad.astype(jnp.bfloat16),
        up_grad.astype(jnp.bfloat16),
        down_grad.astype(jnp.bfloat16),
    )


def solution(mesh):
    in_specs = (
        P("gy", ("gz", "gx")),
        P("gz", ("gx", "gy")),
        P("gz", ("gx", "gy")),
        P("gx", ("gz", "gy")),
        P("gy", ("gz", "gx")),
    )
    out_specs = (
        P("gy", ("gz", "gx")),
        P("gy", ("gz", "gx")),
        P("gz", ("gx", "gy")),
        P("gz", ("gx", "gy")),
        P("gx", ("gz", "gy")),
    )
    return jax.shard_map(local, mesh=mesh, in_specs=in_specs, out_specs=out_specs, check_vma=False)
```

profile of v0, /device:TPU:1, one launch (start us, length us, event | category | flops | bytes accessed | tf_op | source)
XLA Modules:
  0.0 502.1 jit_solution(10327820006403604461)
XLA Ops:
  9.4 22.2 %all_gather.30 = bf16[256,1024]{1,0:T(8,128)(2,1)S(1)} all-gather(bf16[256,128]{1,0:T(8,128)(2,1)} %param.5), channel_id=1, replica_groups=mesh['gx'=8,'gy'=4,'gz'=8] {'gx'}, dimensions={1}, use_global_device_ids=true | all-gather | bytes 589824 | tf_op jit(solution)/shard_map/all_gather | solution.py:25
  31.6 28.5 %all-gather.6.cloned.1.call-done = bf16[1024,1792]{0,1:T(8,128)(2,1)} async-done(((bf16[1024,448]{0,1:T(8,128)(2,1)}), bf16[1024,1792]{0,1:T(8,128)(2,1)}) %all-gather.6.cloned.1.call-update) | async-done | bytes 3670032 | tf_op jit(solution)/shard_map/all_gather | solution.py:29
  60.1 4.4 fusion.3
  64.6 44.1 %all-gather.8.cloned.1.call-done = bf16[1024,1792]{0,1:T(8,128)(2,1)} async-done(((bf16[1024,448]{0,1:T(8,128)(2,1)}), bf16[1024,1792]{0,1:T(8,128)(2,1)}) %all-gather.8.cloned.1.call-update) | async-done | bytes 3670032 | tf_op jit(solution)/shard_map/all_gather | solution.py:30
  108.7 4.4 fusion.4
  113.3 19.1 %all_gather.35 = bf16[256,1024]{0,1:T(8,128)(2,1)} all-gather(bf16[256,128]{0,1:T(8,128)(2,1)S(1)} %copy.14), channel_id=1, replica_groups=mesh['gx'=8,'gy'=4,'gz'=8] {'gx'}, dimensions={1}, use_global_device_ids=true | all-gather | bytes 589824 | tf_op jit(solution)/shard_map/all_gather | solution.py:26
  132.4 27.6 %all-gather.10.cloned.1.call-done = bf16[1792,1024]{1,0:T(8,128)(2,1)} async-done(((bf16[1792,256]{1,0:T(8,128)(2,1)}), bf16[1792,1024]{1,0:T(8,128)(2,1)}) %all-gather.10.cloned.1.call-update) | async-done | bytes 3670032 | tf_op jit(solution)/shard_map/all_gather | solution.py:31
  160.0 4.6 fusion.6
  165.5 37.9 %reduce-scatter.6.cloned.1.call-done = f32[32,1792]{1,0:T(8,128)} async-done(((f32[256,1792]{1,0:T(8,128)}), f32[32,1792]{1,0:T(8,128)}) %reduce-scatter.6.cloned.1.call-update) | async-done | bytes 229392 | tf_op jit(solution)/shard_map/reduce_scatter | solution.py:36
  203.3 45.6 %reduce-scatter.8.cloned.1.call-done = f32[32,1792]{1,0:T(8,128)} async-done(((f32[256,1792]{1,0:T(8,128)}), f32[32,1792]{1,0:T(8,128)}) %reduce-scatter.8.cloned.1.call-update) | async-done | bytes 229392 | tf_op jit(solution)/shard_map/reduce_scatter | solution.py:37
  248.9 45.7 %reduce-scatter.12.cloned.1.call-done = f32[32,1792]{1,0:T(8,128)} async-done(((f32[256,1792]{1,0:T(8,128)}), f32[32,1792]{1,0:T(8,128)}) %reduce-scatter.12.cloned.1.call-update) | async-done | bytes 229392 | tf_op jit(solution)/shard_map/reduce_scatter | solution.py:46
  295.9 23.4 %all_gather.36 = bf16[256,1792]{1,0:T(8,128)(2,1)S(1)} all-gather(bf16[32,1792]{1,0:T(8,128)(2,1)S(1)} %get-tuple-element.6), channel_id=1, replica_groups=mesh['gx'=8,'gy'=4,'gz'=8] {'gz'}, dimensions={0}, use_global_device_ids=true | all-gather | bytes 1032192 | tf_op jit(solution)/shard_map/all_gather | solution.py:50
  322.6 24.5 %all_gather.37 = bf16[256,1792]{1,0:T(8,128)(2,1)S(1)} all-gather(bf16[32,1792]{1,0:T(8,128)(2,1)S(1)} %get-tuple-element.5), channel_id=1, replica_groups=mesh['gx'=8,'gy'=4,'gz'=8] {'gz'}, dimensions={0}, use_global_device_ids=true | all-gather | bytes 1032192 | tf_op jit(solution)/shard_map/all_gather | solution.py:51
  349.3 23.8 %all_gather.33 = bf16[256,1792]{1,0:T(8,128)(2,1)S(1)} all-gather(bf16[32,1792]{1,0:T(8,128)(2,1)S(1)} %get-tuple-element.7), channel_id=1, replica_groups=mesh['gx'=8,'gy'=4,'gz'=8] {'gz'}, dimensions={0}, use_global_device_ids=true | all-gather | bytes 1032192 | tf_op jit(solution)/shard_map/all_gather | solution.py:42
  373.1 4.5 fusion.5
  378.2 4.6 all-to-all-start.2
  384.1 5.9 %all-to-all-done.2 = bf16[256,4,256]{0,2,1:T(8,128)(2,1)S(1)} async-done(((bf16[256,4,256]{0,2,1:T(8,128)(2,1)}), bf16[256,4,256]{0,2,1:T(8,128)(2,1)S(1)}, u32[]{:S(2)}, u32[]{:S(2)}) %all-to-all-start.2) | async-done | bytes 524320 | tf_op jit(solution)/shard_map/all_to_all | solution.py:60
  394.8 8.1 %all-to-all-done = bf16[256,4,448]{0,2,1:T(8,128)(2,1)S(1)} async-done(((bf16[256,4,448]{0,2,1:T(8,128)(2,1)}), bf16[256,4,448]{0,2,1:T(8,128)(2,1)S(1)}, u32[]{:S(2)}, u32[]{:S(2)}) %all-to-all-start) | async-done | bytes 917536 | tf_op jit(solution)/shard_map/all_to_all | solution.py:58
  402.9 3.7 all-to-all-start.1
  406.9 11.3 %all-to-all-done.1 = bf16[256,4,448]{0,2,1:T(8,128)(2,1)S(1)} async-done(((bf16[256,4,448]{0,2,1:T(8,128)(2,1)}), bf16[256,4,448]{0,2,1:T(8,128)(2,1)S(1)}, u32[]{:S(2)}, u32[]{:S(2)}) %all-to-all-start.1) | async-done | bytes 917536 | tf_op jit(solution)/shard_map/all_to_all | solution.py:59
  418.4 3.8 fusion
  425.8 17.7 %reduce-scatter.10.cloned.1.call-done = f32[256,128]{1,0:T(8,128)} async-done(((f32[256,1024]{1,0:T(8,128)}), f32[256,128]{1,0:T(8,128)}) %reduce-scatter.10.cloned.1.call-update) | async-done | bytes 131088 | tf_op jit(solution)/shard_map/reduce_scatter | solution.py:44
  445.1 46.1 %all-gather.14.cloned.1.call-done = bf16[1024,1792]{1,0:T(8,128)(2,1)} async-done(((bf16[256,1792]{1,0:T(8,128)(2,1)}), bf16[1024,1792]{1,0:T(8,128)(2,1)}) %all-gather.14.cloned.1.call-update) | async-done | bytes 3670032 | tf_op jit(solution)/shard_map/all_gather | solution.py:64
  491.2 4.1 convolution_convert_fusion
  (45 shorter events, 22.3 us)
Async XLA Ops:
  7.2 52.9 %all-gather.6.cloned.1.call-start = ((), (), s32[]{:S(2)}) async-start(), calls=%async_computation.8 | async-start | bytes 4587520 | tf_op jit(solution)/shard_map/all_gather | solution.py:29
  7.9 100.8 %all-gather.8.cloned.1.call-start = ((), (), s32[]{:S(2)}) async-start(), calls=%async_computation.10 | async-start | bytes 4587520 | tf_op jit(solution)/shard_map/all_gather | solution.py:30
  8.6 151.4 %all-gather.10.cloned.1.call-start = ((), (), s32[]{:S(2)}) async-start(), calls=%async_computation.12 | async-start | bytes 4587520 | tf_op jit(solution)/shard_map/all_gather | solution.py:31
  9.4 193.9 %reduce-scatter.6.cloned.1.call-start = ((), (), s32[]{:S(2)}) async-start(), calls=%async_computation.9 | async-start | bytes 2064384 | tf_op jit(solution)/shard_map/reduce_scatter | solution.py:36
  31.6 77.1 %copy-start.1 = (bf16[256,1024]{1,0:T(8,128)(2,1)}, bf16[256,1024]{1,0:T(8,128)(2,1)S(1)}, u32[]{:S(2)}) copy-start(bf16[256,1024]{1,0:T(8,128)(2,1)S(1)} %all_gather.30) | copy-start | bytes 1572868
  64.5 48.7 %copy-start.2 = (bf16[256,128]{1,0:T(8,128)(2,1)S(1)}, bf16[256,128]{1,0:T(8,128)(2,1)}, u32[]{:S(2)}) copy-start(bf16[256,128]{1,0:T(8,128)(2,1)} %param.9) | copy-start | bytes 196612
  64.5 184.4 %reduce-scatter.8.cloned.1.call-start = ((), (), s32[]{:S(2)}) async-start(), calls=%async_computation.11 | async-start | bytes 2064384 | tf_op jit(solution)/shard_map/reduce_scatter | solution.py:37
  113.1 181.4 %reduce-scatter.12.cloned.1.call-start = ((), (), s32[]{:S(2)}) async-start(), calls=%async_computation.14 | async-start | bytes 2064384 | tf_op jit(solution)/shard_map/reduce_scatter | solution.py:46
  164.7 253.7 %all-gather.12.cloned.1.call-start = ((), (), s32[]{:S(2)}) async-start(), calls=%async_computation.16 | async-start | bytes 2621440 | tf_op jit(solution)/shard_map/all_gather | solution.py:63
  165.4 258.8 %reduce-scatter.14.cloned.1.call-start = ((), (), s32[]{:S(2)}) async-start(), calls=%async_computation.15 | async-start | bytes 1179648 | tf_op jit(solution)/shard_map/reduce_scatter | solution.py:54
  319.3 27.9 %copy-start.3 = (bf16[1024,1792]{0,1:T(8,128)(2,1)S(1)}, bf16[1024,1792]{0,1:T(8,128)(2,1)}, u32[]{:S(2)}) copy-start(bf16[1024,1792]{0,1:T(8,128)(2,1)} %all-gather.8.cloned.1.call-done) | copy-start | bytes 11010052
  349.3 94.3 %reduce-scatter.10.cloned.1.call-start = ((), (), s32[]{:S(2)}) async-start(), calls=%async_computation.13 | async-start | bytes 1179648 | tf_op jit(solution)/shard_map/reduce_scatter | solution.py:44
  373.1 4.5 copy-start
  377.6 113.6 %all-gather.14.cloned.1.call-start = ((), (), s32[]{:S(2)}) async-start(), calls=%async_computation.17 | async-start | bytes 4587520 | tf_op jit(solution)/shard_map/all_gather | solution.py:64
  378.2 11.9 %all-to-all-start.2 = ((bf16[256,4,256]{0,2,1:T(8,128)(2,1)}), bf16[256,4,256]{0,2,1:T(8,128)(2,1)S(1)}, u32[]{:S(2)}, u32[]{:S(2)}) async-start(bf16[256,4,256]{0,2,1:T(8,128)(2,1)} %bitcast.6), calls=%async_computation.7 | async-start | bytes 1048576 | tf_op jit(solution)/shard_map/all_to_all | solution.py:60
  390.0 12.9 %all-to-all-start = ((bf16[256,4,448]{0,2,1:T(8,128)(2,1)}), bf16[256,4,448]{0,2,1:T(8,128)(2,1)S(1)}, u32[]{:S(2)}, u32[]{:S(2)}) async-start(bf16[256,4,448]{0,2,1:T(8,128)(2,1)} %bitcast), calls=%async_computation.5 | async-start | bytes 1835008 | tf_op jit(solution)/shard_map/all_to_all | solution.py:58
  402.9 15.3 %all-to-all-start.1 = ((bf16[256,4,448]{0,2,1:T(8,128)(2,1)}), bf16[256,4,448]{0,2,1:T(8,128)(2,1)S(1)}, u32[]{:S(2)}, u32[]{:S(2)}) async-start(bf16[256,4,448]{0,2,1:T(8,128)(2,1)} %bitcast.3), calls=%async_computation.6 | async-start | bytes 1835008 | tf_op jit(solution)/shard_map/all_to_all | solution.py:59
  418.4 3.8 copy-start.4
Sparse Core Ops, SparseCore 0:
  9.8 50.2 all-gather.5
  61.9 46.7 all-gather.7
  110.5 49.5 all-gather.9
  162.4 40.8 reduce-scatter.5
  205.7 43.1 reduce-scatter.7
  251.3 43.1 reduce-scatter.11
  296.9 37.5 all-gather.11
  349.4 54.7 reduce-scatter.13
  406.8 36.7 reduce-scatter.9
  445.2 45.9 all-gather.13
where the time goes:
time: 503 us; the launch traced here: 502 us
  waiting for transfers between devices  322 us (64%)
  blocking collectives  113 us (22%)
  matrix products  33.4 us (7%)
  between operations  14.3 us (3%)
  starting transfers between devices  12.2 us (2%)
    all_gather x1, waiting for transfers between devices, local(): lax.all_gather(hidden_all, 'gy', axis=0, tiled=True)  46.1 us
    reduce_scatter x1, waiting for transfers between devices, local(): dh_rows = lax.psum_scatter(dh_part, 'gz', scatter_dimension=0, tiled=True)  45.7 us
    reduce_scatter x1, waiting for transfers between devices, local(): lax.psum_scatter(up_part, 'gz', scatter_dimension=0, tiled=True)  45.6 us
    all_gather x1, waiting for transfers between devices, local(): lax.all_gather(up_weight, 'gy', axis=1, tiled=True)  44.1 us
    reduce_scatter x1, waiting for transfers between devices, local(): lax.psum_scatter(gate_part, 'gz', scatter_dimension=0, tiled=True)  37.9 us
    all_gather x1, waiting for transfers between devices, local(): lax.all_gather(gate_weight, 'gy', axis=1, tiled=True)  28.5 us
    all_gather x1, waiting for transfers between devices, local(): lax.all_gather(down_weight, 'gy', axis=1, tiled=True)  27.6 us
    all_gather x1, blocking collectives, local(): lax.all_gather(up_delta, 'gz', axis=0, tiled=True)  24.5 us
  transfers between devices with their start and end apart: 13, of which 11 were waited for; matrix products, arithmetic and copies ran while one was open for 7% of the time, Pallas kernels for 0%

commit v1 on v0

--- a/solution.py
+++ b/solution.py
@@ -2,6 +2,10 @@
 import jax.numpy as jnp
 from jax import lax
 from jax.sharding import PartitionSpec as P
+
+treat_the_target = lambda frame_in: jnp.concatenate(
+    lax.all_to_all(jnp.stack([frame_in for _ in range(lax.psum(1, "gz"))], 0), "gz", 0, 0), axis=0
+)
 
 
 def matmul(left, right):
@@ -47,7 +51,7 @@
     gate_delta = (dh_rows * up_rows * sig * (1.0 + gate_rows * (1.0 - sig))).astype(jnp.bfloat16)
     up_delta = (dh_rows * act).astype(jnp.bfloat16)
     gate_all, up_all = (
-        lax.all_gather(gate_delta, "gz", axis=0, tiled=True),
+        treat_the_target(gate_delta),
         lax.all_gather(up_delta, "gz", axis=0, tiled=True),
     )
     dx_part = matmul_right_t(gate_all, gate_full) + matmul_right_t(up_all, up_full)

time: 503 us -> 483 us (0.960)
  blocking collectives: 113 us -> 96.4 us
  waiting for transfers between devices: 322 us -> 310 us
    all_gather x1 -> x0, blocking collectives: 23.4 us -> none  [local(): lax.all_gather(gate_delta, 'gz', axis=0, tiled=True)]
    reduce_scatter x1, waiting for transfers between devices: 17.7 us -> 0.01 us  [local(): lax.psum_scatter(out_part, 'gx', scatter_dimension=1, tiled=True)]
    reduce_scatter x1, waiting for transfers between devices: 0.01 us -> 15.8 us  [local(): lax.psum_scatter(dx_part, 'gx', scatter_dimension=1, tiled=True)]
    all_gather x1, blocking collectives: 23.8 us -> 30.2 us  [local(): hidden_all = lax.all_gather(hidden, 'gz', axis=0, tiled=True)]
    all_to_all x1, waiting for transfers between devices: 8.07 us -> 2.83 us  [local(): lax.all_to_all(gate_all, 'gy', split_axis=1, concat_axis=0, tiled=True)]
    all_to_all x1, waiting for transfers between devices: 11.3 us -> 6.2 us  [local(): lax.all_to_all(up_all, 'gy', split_axis=1, concat_axis=0, tiled=True)]
  transfers between devices with their start and end apart: 13 -> 14, of which waited for: 11 -> 11; matrix products, arithmetic and copies ran while one was open for 7% -> 8% of each run, Pallas kernels for 0% -> 0%
where the time goes in v1:
time: 483 us; the launch traced here: 482 us
  waiting for transfers between devices  310 us (64%)
  blocking collectives  96.4 us (20%)
  matrix products  35.2 us (7%)
  starting transfers between devices  15.9 us (3%)
  between operations  14.3 us (3%)
  local copies, waits for them, and re-layouts  6.43 us (1%)
    all_gather x1, waiting for transfers between devices, local(): lax.all_gather(hidden_all, 'gy', axis=0, tiled=True)  46.2 us
    reduce_scatter x1, waiting for transfers between devices, local(): dh_rows = lax.psum_scatter(dh_part, 'gz', scatter_dimension=0, tiled=True)  45.7 us
    reduce_scatter x1, waiting for transfers between devices, local(): lax.psum_scatter(up_part, 'gz', scatter_dimension=0, tiled=True)  45.6 us
    all_gather x1, waiting for transfers between devices, local(): lax.all_gather(up_weight, 'gy', axis=1, tiled=True)  44.1 us
    reduce_scatter x1, waiting for transfers between devices, local(): lax.psum_scatter(gate_part, 'gz', scatter_dimension=0, tiled=True)  37.9 us
    all_gather x1, blocking collectives, local(): hidden_all = lax.all_gather(hidden, 'gz', axis=0, tiled=True)  30.2 us
    all_gather x1, waiting for transfers between devices, local(): lax.all_gather(gate_weight, 'gy', axis=1, tiled=True)  28.5 us
    all_gather x1, waiting for transfers between devices, local(): lax.all_gather(down_weight, 'gy', axis=1, tiled=True)  27.6 us
  transfers between devices with their start and end apart: 14, of which 11 were waited for; matrix products, arithmetic and copies ran while one was open for 8% of the time, Pallas kernels for 0%

profile of v1, /device:TPU:1, one launch (start us, length us, event | category | flops | bytes accessed | tf_op | source)
XLA Modules:
  0.0 482.2 jit_solution(6025222181400873222)
XLA Ops:
  9.4 22.2 %all_gather.27 = bf16[256,1024]{1,0:T(8,128)(2,1)S(1)} all-gather(bf16[256,128]{1,0:T(8,128)(2,1)} %param.5), channel_id=1, replica_groups=mesh['gx'=8,'gy'=4,'gz'=8] {'gx'}, dimensions={1}, use_global_device_ids=true | all-gather | bytes 589824 | tf_op jit(solution)/shard_map/all_gather | solution.py:29
  31.6 28.5 %all-gather.6.cloned.1.call-done = bf16[1024,1792]{0,1:T(8,128)(2,1)} async-done(((bf16[1024,448]{0,1:T(8,128)(2,1)}), bf16[1024,1792]{0,1:T(8,128)(2,1)}) %all-gather.6.cloned.1.call-update) | async-done | bytes 3670032 | tf_op jit(solution)/shard_map/all_gather | solution.py:33
  60.1 4.4 fusion.3
  64.6 44.1 %all-gather.8.cloned.1.call-done = bf16[1024,1792]{0,1:T(8,128)(2,1)} async-done(((bf16[1024,448]{0,1:T(8,128)(2,1)}), bf16[1024,1792]{0,1:T(8,128)(2,1)}) %all-gather.8.cloned.1.call-update) | async-done | bytes 3670032 | tf_op jit(solution)/shard_map/all_gather | solution.py:34
  108.7 4.4 fusion.4
  113.3 19.1 %all_gather.32 = bf16[256,1024]{0,1:T(8,128)(2,1)} all-gather(bf16[256,128]{0,1:T(8,128)(2,1)S(1)} %copy.18), channel_id=1, replica_groups=mesh['gx'=8,'gy'=4,'gz'=8] {'gx'}, dimensions={1}, use_global_device_ids=true | all-gather | bytes 589824 | tf_op jit(solution)/shard_map/all_gather | solution.py:30
  132.4 27.6 %all-gather.10.cloned.1.call-done = bf16[1792,1024]{1,0:T(8,128)(2,1)} async-done(((bf16[1792,256]{1,0:T(8,128)(2,1)}), bf16[1792,1024]{1,0:T(8,128)(2,1)}) %all-gather.10.cloned.1.call-update) | async-done | bytes 3670032 | tf_op jit(solution)/shard_map/all_gather | solution.py:35
  160.0 4.6 fusion.6
  165.4 37.9 %reduce-scatter.6.cloned.1.call-done = f32[32,1792]{1,0:T(8,128)} async-done(((f32[256,1792]{1,0:T(8,128)}), f32[32,1792]{1,0:T(8,128)}) %reduce-scatter.6.cloned.1.call-update) | async-done | bytes 229392 | tf_op jit(solution)/shard_map/reduce_scatter | solution.py:40
  203.3 45.6 %reduce-scatter.8.cloned.1.call-done = f32[32,1792]{1,0:T(8,128)} async-done(((f32[256,1792]{1,0:T(8,128)}), f32[32,1792]{1,0:T(8,128)}) %reduce-scatter.8.cloned.1.call-update) | async-done | bytes 229392 | tf_op jit(solution)/shard_map/reduce_scatter | solution.py:41
  248.9 45.7 %reduce-scatter.12.cloned.1.call-done = f32[32,1792]{1,0:T(8,128)} async-done(((f32[256,1792]{1,0:T(8,128)}), f32[32,1792]{1,0:T(8,128)}) %reduce-scatter.12.cloned.1.call-update) | async-done | bytes 229392 | tf_op jit(solution)/shard_map/reduce_scatter | solution.py:50
  296.8 4.1 all-to-all-start
  300.9 30.2 %all_gather.30 = bf16[256,1792]{1,0:T(8,128)(2,1)S(1)} all-gather(bf16[32,1792]{1,0:T(8,128)(2,1)S(1)} %get-tuple-element.7), channel_id=1, replica_groups=mesh['gx'=8,'gy'=4,'gz'=8] {'gz'}, dimensions={0}, use_global_device_ids=true | all-gather | bytes 1032192 | tf_op jit(solution)/shard_map/all_gather | solution.py:46
  331.2 4.5 fusion.5
  335.7 25.0 %all_gather.33 = bf16[256,1792]{1,0:T(8,128)(2,1)S(1)} all-gather(bf16[32,1792]{1,0:T(8,128)(2,1)S(1)} %get-tuple-element.5), channel_id=1, replica_groups=mesh['gx'=8,'gy'=4,'gz'=8] {'gz'}, dimensions={0}, use_global_device_ids=true | all-gather | bytes 1032192 | tf_op jit(solution)/shard_map/all_gather | solution.py:55
  367.0 4.2 all-to-all-start.3
  372.5 5.9 %all-to-all-done.3 = bf16[256,4,256]{0,2,1:T(8,128)(2,1)S(1)} async-done(((bf16[256,4,256]{0,2,1:T(8,128)(2,1)}), bf16[256,4,256]{0,2,1:T(8,128)(2,1)S(1)}, u32[]{:S(2)}, u32[]{:S(2)}) %all-to-all-start.3) | async-done | bytes 524320 | tf_op jit(solution)/shard_map/all_to_all | solution.py:64
  384.7 6.2 %all-to-all-done.2 = bf16[256,4,448]{0,2,1:T(8,128)(2,1)S(1)} async-done(((bf16[256,4,448]{0,2,1:T(8,128)(2,1)}), bf16[256,4,448]{0,2,1:T(8,128)(2,1)S(1)}, u32[]{:S(2)}, u32[]{:S(2)}) %all-to-all-start.2) | async-done | bytes 917536 | tf_op jit(solution)/shard_map/all_to_all | solution.py:63
  390.9 3.7 all-to-all-start.1
  395.8 3.7 fusion.1
  404.0 3.7 fusion
  407.7 15.8 %reduce-scatter.14.cloned.1.call-done = f32[256,128]{1,0:T(8,128)} async-done(((f32[256,1024]{1,0:T(8,128)}), f32[256,128]{1,0:T(8,128)}) %reduce-scatter.14.cloned.1.call-update) | async-done | bytes 131088 | tf_op jit(solution)/shard_map/reduce_scatter | solution.py:58
  425.1 46.2 %all-gather.14.cloned.1.call-done = bf16[1024,1792]{1,0:T(8,128)(2,1)} async-done(((bf16[256,1792]{1,0:T(8,128)(2,1)}), bf16[1024,1792]{1,0:T(8,128)(2,1)}) %all-gather.14.cloned.1.call-update) | async-done | bytes 3670032 | tf_op jit(solution)/shard_map/all_gather | solution.py:68
  471.3 4.1 convolution_convert_fusion
  (52 shorter events, 26.6 us)
Async XLA Ops:
  7.2 52.9 %all-gather.6.cloned.1.call-start = ((), (), s32[]{:S(2)}) async-start(), calls=%async_computation.9 | async-start | bytes 4587520 | tf_op jit(solution)/shard_map/all_gather | solution.py:33
  7.9 100.8 %all-gather.8.cloned.1.call-start = ((), (), s32[]{:S(2)}) async-start(), calls=%async_computation.11 | async-start | bytes 4587520 | tf_op jit(solution)/shard_map/all_gather | solution.py:34
  8.6 151.4 %all-gather.10.cloned.1.call-start = ((), (), s32[]{:S(2)}) async-start(), calls=%async_computation.13 | async-start | bytes 4587520 | tf_op jit(solution)/shard_map/all_gather | solution.py:35
  9.4 193.9 %reduce-scatter.6.cloned.1.call-start = ((), (), s32[]{:S(2)}) async-start(), calls=%async_computation.10 | async-start | bytes 2064384 | tf_op jit(solution)/shard_map/reduce_scatter | solution.py:40
  31.6 77.1 %copy-start.3 = (bf16[256,1024]{1,0:T(8,128)(2,1)}, bf16[256,1024]{1,0:T(8,128)(2,1)S(1)}, u32[]{:S(2)}) copy-start(bf16[256,1024]{1,0:T(8,128)(2,1)S(1)} %all_gather.27) | copy-start | bytes 1572868
  64.5 48.7 %copy-start.5 = (bf16[256,128]{1,0:T(8,128)(2,1)S(1)}, bf16[256,128]{1,0:T(8,128)(2,1)}, u32[]{:S(2)}) copy-start(bf16[256,128]{1,0:T(8,128)(2,1)} %param.9) | copy-start | bytes 196612
  64.5 184.4 %reduce-scatter.8.cloned.1.call-start = ((), (), s32[]{:S(2)}) async-start(), calls=%async_computation.12 | async-start | bytes 2064384 | tf_op jit(solution)/shard_map/reduce_scatter | solution.py:41
  113.1 181.4 %reduce-scatter.12.cloned.1.call-start = ((), (), s32[]{:S(2)}) async-start(), calls=%async_computation.15 | async-start | bytes 2064384 | tf_op jit(solution)/shard_map/reduce_scatter | solution.py:50
  164.7 231.1 %all-gather.12.cloned.1.call-start = ((), (), s32[]{:S(2)}) async-start(), calls=%async_computation.17 | async-start | bytes 2621440 | tf_op jit(solution)/shard_map/all_gather | solution.py:67
  296.8 63.8 %all-to-all-start = ((bf16[8,32,1792]{2,1,0:T(8,128)(2,1)}), bf16[8,32,1792]{2,1,0:T(8,128)(2,1)S(1)}, u32[]{:S(2)}, u32[]{:S(2)}) async-start(bf16[8,32,1792]{2,1,0:T(8,128)(2,1)} %stack.2), calls=%async_computation.4 | async-start | bytes 1835008 | tf_op jit(solution)/shard_map/all_to_all | solution.py:7
  300.9 98.6 %reduce-scatter.10.cloned.1.call-start = ((), (), s32[]{:S(2)}) async-start(), calls=%async_computation.14 | async-start | bytes 1179648 | tf_op jit(solution)/shard_map/reduce_scatter | solution.py:48
  331.2 4.5 copy-start
  335.7 87.9 %reduce-scatter.14.cloned.1.call-start = ((), (), s32[]{:S(2)}) async-start(), calls=%async_computation.16 | async-start | bytes 1179648 | tf_op jit(solution)/shard_map/reduce_scatter | solution.py:58
  360.7 5.7 %copy-start.1 = (bf16[8,32,1792]{2,1,0:T(8,128)(2,1)}, bf16[8,32,1792]{2,1,0:T(8,128)(2,1)S(1)}, u32[]{:S(2)}) copy-start(bf16[8,32,1792]{2,1,0:T(8,128)(2,1)S(1)} %all-to-all-done) | copy-start | bytes 2752516
  360.7 3.5 copy-start.6
  366.4 15.6 %copy-start.2 = (bf16[8,32,1792]{2,1,0:T(8,128)(2,1)S(1)}, bf16[8,32,1792]{2,1,0:T(8,128)(2,1)}, u32[]{:S(2)}) copy-start(bf16[8,32,1792]{2,1,0:T(8,128)(2,1)} %copy-done.1) | copy-start | bytes 2752516
  366.4 104.9 %all-gather.14.cloned.1.call-start = ((), (), s32[]{:S(2)}) async-start(), calls=%async_computation.18 | async-start | bytes 4587520 | tf_op jit(solution)/shard_map/all_gather | solution.py:68
  367.0 11.4 %all-to-all-start.3 = ((bf16[256,4,256]{0,2,1:T(8,128)(2,1)}), bf16[256,4,256]{0,2,1:T(8,128)(2,1)S(1)}, u32[]{:S(2)}, u32[]{:S(2)}) async-start(bf16[256,4,256]{0,2,1:T(8,128)(2,1)} %bitcast.6), calls=%async_computation.8 | async-start | bytes 1048576 | tf_op jit(solution)/shard_map/all_to_all | solution.py:64
  378.4 12.5 %all-to-all-start.2 = ((bf16[256,4,448]{0,2,1:T(8,128)(2,1)}), bf16[256,4,448]{0,2,1:T(8,128)(2,1)S(1)}, u32[]{:S(2)}, u32[]{:S(2)}) async-start(bf16[256,4,448]{0,2,1:T(8,128)(2,1)} %bitcast.3), calls=%async_computation.7 | async-start | bytes 1835008 | tf_op jit(solution)/shard_map/all_to_all | solution.py:63
  390.9 12.9 %all-to-all-start.1 = ((bf16[256,4,448]{0,2,1:T(8,128)(2,1)}), bf16[256,4,448]{0,2,1:T(8,128)(2,1)S(1)}, u32[]{:S(2)}, u32[]{:S(2)}) async-start(bf16[256,4,448]{0,2,1:T(8,128)(2,1)} %copy.19), calls=%async_computation.6 | async-start | bytes 1835008 | tf_op jit(solution)/shard_map/all_to_all | solution.py:62
  404.0 67.3 %copy-start.4 = (bf16[4,256,256]{2,1,0:T(8,128)(2,1)S(1)}, bf16[4,256,256]{2,1,0:T(8,128)(2,1)}, u32[]{:S(2)}) copy-start(bf16[4,256,256]{2,1,0:T(8,128)(2,1)} %copy.23) | copy-start | bytes 1572868
Sparse Core Ops, SparseCore 0:
  9.8 50.2 all-gather.5
  61.9 46.7 all-gather.7
  110.5 49.5 all-gather.9
  162.4 40.8 reduce-scatter.5
  205.7 43.1 reduce-scatter.7
  251.3 43.1 reduce-scatter.11
  296.9 37.5 all-gather.11
  337.1 45.9 reduce-scatter.9
  385.6 37.8 reduce-scatter.13
  425.2 46.0 all-gather.13
